TPU v7x, 32 devices: a whole 2x2x4 slice. The times are simulated.
32 devices in a mesh: leaf: 8 (over y, x, core), probe: 4 (over z).
Axes of the slice: x: 2, y: 2, z: 4, core: 2. Of those that a mesh axis runs over, the one named last changes fastest.
Arguments:
- points: bfloat16 [32768, 2048], P('leaf', 'probe'), parts along dimension 1, may hold values from -6 to 6
- leaf_basis: bfloat16 [128, 64, 256], P('leaf'), may hold values from -0.375 to 0.375
- local_transfer: bfloat16 [240, 4096], P('leaf'), may hold values from -0.5 to 0.5
- top_transfer: bfloat16 [14, 4096], replicated, may hold values from -0.5 to 0.5
- sources: int32 [8184], P('leaf'), may hold values from 0 to 127, as said below
- couplings: bfloat16 [8184, 4096], P('leaf'), as said below
Outputs:
- coupled: bfloat16 [248, 64, 2048], P('leaf', None, 'probe'), parts along dimension 2
- ancestors: bfloat16 [8, 3, 64, 2048], P('leaf', None, None, 'probe'), parts along dimension 3
There are 4 independent parts, one for each index of `probe`. A program takes and returns all parts, laid end to end along the dimension named above; an argument that names none is the same for every part. Nothing has to cross between parts.
Inputs may be any that keep to these rules, and one draw needn't show every extreme that they name: `sources`: each entry names a cluster of its target's level lying in the target's subtree or in one of the two subtrees on either side; the entries of one target are distinct. `couplings`: tiles of level h have entries of deviation (3 * 64 * 16 / 2^h)^(-1/2).
All inputs are finite; a program needn't handle non-finite values.
Results may differ from a plain program's by a relative error of at most 0.0095.
Values may be sent and summed in bfloat16 or wider, within the bound.
A program may use at most 128 MiB of HBM per device.

v0:
```python
import jax
import jax.numpy as jnp
from jax import lax
from jax.sharding import PartitionSpec as P

LEAF = 256
RANK = 64
PROBES = 512
LOCAL = 5
LEAF_DEV = 16


def from_behind(block, axis, distance):
    devices = range(lax.axis_size(axis))
    route = [(i - distance, i) for i in devices if i - distance in devices]
    return lax.ppermute(block, axis, route)


def partner(value, axis, distance):
    mask = 2**distance
    pairs = [(source, source ^ mask) for source in range(lax.axis_size(axis))]
    return lax.ppermute(value, axis, pairs)


def lift_level(children, matrices):
    shaped = matrices.reshape(-1, RANK, RANK)
    products = jnp.einsum("cab,cap->cbp", shaped, children, preferred_element_type=jnp.float32)
    return products.reshape(-1, 2, RANK, PROBES).sum(axis=1)


def couple_level(window, level_sources, level_tiles, anchor, number):
    local_index = (level_sources - anchor).reshape(number, 3 * number)
    slots = jnp.arange(5 * number, dtype=jnp.int32)
    selector = (local_index[:, :, None] == slots[None, None, :]).astype(jnp.bfloat16)
    tiles = level_tiles.reshape(number, 3 * number, RANK * RANK)
    placed = jnp.einsum("tks,tkm->tsm", selector, tiles, preferred_element_type=jnp.float32)
    dense = placed.astype(jnp.bfloat16).reshape(number, 5 * number, RANK, RANK)
    summed = jnp.einsum("tsab,sap->tbp", dense, window, preferred_element_type=jnp.float32)
    return summed.astype(jnp.bfloat16)


def joint_window(joined):
    pieces = []
    for distance in (2, 1, 0, -1, -2):
        if distance == 0:
            pieces.append(joined)
        else:
            pieces.append(from_behind(joined, "leaf", distance))
    return pieces


def shards(points, leaf_basis, local_transfer, top_transfer, sources, couplings):
    device = lax.axis_index("leaf")
    subtrees = lax.axis_size("leaf")
    levels_up = subtrees.bit_length() - 1
    blocks = points.reshape(LEAF_DEV, LEAF, PROBES)
    first = jnp.einsum("jrl,jlp->jrp", leaf_basis, blocks, preferred_element_type=jnp.float32)
    moments = [first.astype(jnp.bfloat16)]
    cursor = 0
    for height in range(1, LOCAL):
        number = LEAF_DEV >> height - 1
        lifted = lift_level(moments[-1], local_transfer[cursor : cursor + number])
        moments.append(lifted.astype(jnp.bfloat16))
        cursor += number
    windows = []
    received = joint_window(jnp.concatenate(moments, axis=0))
    cursor = 0
    for height in range(LOCAL):
        number = LEAF_DEV >> height
        windows.append(
            jnp.concatenate([piece[cursor : cursor + number] for piece in received], axis=0)
        )
        cursor += number
    outputs = []
    cursor = 0
    for height in range(LOCAL):
        number = LEAF_DEV >> height
        entries = 3 * number * number
        anchor = (device - 2) * number
        outputs.append(
            couple_level(
                windows[height],
                sources[cursor : cursor + entries],
                couplings[cursor : cursor + entries],
                anchor,
                number,
            )
        )
        cursor += entries
    coupled = jnp.concatenate(outputs, axis=0)
    device_root = moments[LOCAL - 1]
    ladder = []
    current = device_root[0]
    cursor = 0
    for height in range(levels_up):
        row = cursor + (device >> height)
        matrix = lax.dynamic_index_in_dim(top_transfer, row, 0, keepdims=False).reshape(RANK, RANK)
        portion = jnp.einsum("ab,ap->bp", matrix, current, preferred_element_type=jnp.float32)
        sibling_part = partner(portion, "leaf", height)
        current = (portion + sibling_part).astype(jnp.bfloat16)
        ladder.append(current)
        cursor += subtrees >> height
    ancestors = jnp.stack(ladder, axis=0)[None]
    return (coupled, ancestors)


def solution(mesh):
    placed = (
        P("leaf", "probe"),
        P("leaf", None, None),
        P("leaf", None),
        P(),
        P("leaf"),
        P("leaf", None),
    )
    return jax.shard_map(
        shards,
        mesh=mesh,
        in_specs=placed,
        out_specs=(P("leaf", None, "probe"), P("leaf", None, None, "probe")),
        check_vma=False,
    )
```

profile of v0, /device:TPU:0, one launch (start us, length us, event | category | flops | bytes accessed | tf_op | source)
XLA Modules:
  0.0 194.9 jit_solution(9008868601335352693)
XLA Ops:
  3.8 4.0 %constant_dynamic-update-slice_fusion.4 = (bf16[31,64,512]{2,1,0:T(8,128)(2,1)}, bf16[16,64,512]{2,1,0:T(8,128)(2,1)S(1)}) fusion(bf16[16,64,256]{2,1,0:T(8,128)(2,1)S(1)} %copy-done, bf16[16,256,512]{2,1,0:T(8,128)(2,1)} %bitcast.138), kind=kOutput, calls=%fused_computation.60 | convolution fusion | flops 268959744 | bytes 6815744 | tf_op jit(solution)/shard_map/jrl,jlp->jrp/dot_general | solution.py:57
  13.2 6.2 %collective-permute-start = (bf16[31,64,512]{2,1,0:T(8,128)(2,1)}, bf16[31,64,512]{2,1,0:T(8,128)(2,1)}, u32[]{:S(2)}, u32[]{:S(2)}) collective-permute-start(bf16[31,64,512]{2,1,0:T(8,128)(2,1)} %get-tuple-element.7), channel_id=1, source_target_pairs={{0,8},{4,12},{8,16},{12,20},{16,24},{20,28},{1,9},{5,13},{9,17},{1... | collective-permute-start | bytes 6094856 | tf_op jit(solution)/shard_map/ppermute | solution.py:16
  19.4 2.7 %collective-permute-start.1 = (bf16[31,64,512]{2,1,0:T(8,128)(2,1)}, bf16[31,64,512]{2,1,0:T(8,128)(2,1)}, u32[]{:S(2)}, u32[]{:S(2)}) collective-permute-start(bf16[31,64,512]{2,1,0:T(8,128)(2,1)} %get-tuple-element.7), channel_id=1, source_target_pairs={{0,4},{4,8},{8,12},{12,16},{16,20},{20,24},{24,28},{1,5},{5,9},{9,... | collective-permute-start | bytes 6094856 | tf_op jit(solution)/shard_map/ppermute | solution.py:16
  22.1 1.3 collective-permute-start.2
  23.4 1.3 collective-permute-start.3
  26.7 1.1 collective-permute-start.4
  27.8 6.2 %slice.103 = bf16[768,4096]{1,0:T(8,128)(2,1)} slice(bf16[1023,4096]{1,0:T(8,128)(2,1)} %param.11), slice={[0:768], [0:4096]} | slice | bytes 12582912 | tf_op jit(solution)/shard_map/slice | solution.py:84
  37.1 9.9 %convolution_convert_fusion = bf16[16,80,4096]{2,1,0:T(8,128)(2,1)} fusion(bf16[16,48,4096]{2,1,0:T(8,128)(2,1)} %bitcast.134, s32[16,48]{1,0:T(8,128)S(1)} %sub.68), kind=kOutput, calls=%fused_computation | convolution fusion | flops 508620800 | bytes 16780288 | tf_op jit(solution)/shard_map/tks,tkm->tsm/dot_general | solution.py:36
  48.1 1.5 convolution_convert_fusion.2
  50.4 18.2 %copy.40 = bf16[16,80,4096]{1,2,0:T(8,128)(2,1)} copy(bf16[16,80,4096]{2,1,0:T(8,128)(2,1)} %convolution_convert_fusion) | data formatting | bytes 20971520 | tf_op jit(solution)/shard_map/reshape | solution.py:37
  68.5 36.5 %copy.30 = bf16[16,80,64,64]{3,2,1,0:T(8,128)(2,1)} copy(bf16[16,80,64,64]{1,3,2,0:T(8,128)(2,1)} %bitcast.133) | data formatting | bytes 20971520 | tf_op jit(solution)/shard_map/reshape | solution.py:37
  105.0 6.7 %reshape.154 = bf16[8,40,64,64]{3,2,1,0:T(8,128)(2,1)} reshape(bf16[8,40,4096]{2,1,0:T(8,128)(2,1)S(1)} %convolution_convert_fusion.1) | data formatting | bytes 5242880 | tf_op jit(solution)/shard_map/reshape | solution.py:37
  111.7 2.4 %reshape.173 = bf16[4,20,64,64]{3,2,1,0:T(8,128)(2,1)S(1)} reshape(bf16[4,20,4096]{2,1,0:T(8,128)(2,1)} %convolution_convert_fusion.2) | data formatting | bytes 1310720 | tf_op jit(solution)/shard_map/reshape | solution.py:37
  117.0 2.4 %collective-permute-start.5 = (f32[64,512]{1,0:T(8,128)S(1)}, f32[64,512]{1,0:T(8,128)S(1)}, u32[]{:S(2)}, u32[]{:S(2)}) collective-permute-start(f32[64,512]{1,0:T(8,128)S(1)} %fusion.53), channel_id=1, source_target_pairs={{0,8},{4,12},{8,0},{12,4},{16,24},{20,28},{24,16},{28,20},{1,9},{5... | collective-permute-start | bytes 393224 | tf_op jit(solution)/shard_map/ppermute | solution.py:22
  120.2 33.4 %collective-permute-done.5 = f32[64,512]{1,0:T(8,128)S(1)} collective-permute-done((f32[64,512]{1,0:T(8,128)S(1)}, f32[64,512]{1,0:T(8,128)S(1)}, u32[]{:S(2)}, u32[]{:S(2)}) %collective-permute-start.5) | collective-permute-done | bytes 131104 | tf_op jit(solution)/shard_map/ppermute | solution.py:22
  153.8 1.1 convolution_convert_fusion.4
  155.7 3.1 %collective-permute-done.6 = f32[64,512]{1,0:T(8,128)S(1)} collective-permute-done((f32[64,512]{1,0:T(8,128)S(1)}, f32[64,512]{1,0:T(8,128)S(1)}, u32[]{:S(2)}, u32[]{:S(2)}) %collective-permute-start.6) | collective-permute-done | bytes 131104 | tf_op jit(solution)/shard_map/ppermute | solution.py:22
  165.7 1.4 slice_dynamic-update-slice_fusion.3
  167.1 1.3 slice_dynamic-update-slice_fusion.2
  170.2 1.3 slice_dynamic-update-slice_fusion.1
  171.5 1.4 slice_dynamic-update-slice_fusion
  173.0 10.2 %fusion.6 = bf16[31,64,512]{2,1,0:T(8,128)(2,1)S(1)} fusion(bf16[16,80,64,64]{3,2,1,0:T(8,128)(2,1)} %copy.30, bf16[80,64,512]{2,1,0:T(8,128)(2,1)S(1)} %slice_dynamic-update-slice_fusion), kind=kOutput, calls=%fused_computation.12 | convolution fusion | flops 5369233408 | bytes 16777216 | tf_op jit(solution)/shard_map/tsab,sap->tbp/dot_general | solution.py:38
  185.4 1.5 fusion.17
  193.6 1.3 copy-done.14
  (112 shorter events, 37.3 us)
Async XLA Ops:
  0.6 3.1 %copy-start = (bf16[16,64,256]{2,1,0:T(8,128)(2,1)S(1)}, bf16[16,64,256]{2,1,0:T(8,128)(2,1)}, u32[]{:S(2)}) copy-start(bf16[16,64,256]{2,1,0:T(8,128)(2,1)} %param.7) | copy-start | bytes 1572868
  7.8 2.7 %slice-start.5 = ((bf16[30,4096]{1,0:T(8,128)(2,1)}), bf16[4,4096]{1,0:T(4,128)(2,1)S(1)}, s32[]{:S(2)}) async-start(bf16[30,4096]{1,0:T(8,128)(2,1)} %param.8), calls=%async_computation.5 | async-start | bytes 65536 | tf_op jit(solution)/shard_map/slice | solution.py:62
  9.2 18.6 %copy-start.4 = (bf16[8,64,512]{2,1,0:T(8,128)(2,1)}, bf16[8,64,512]{2,1,0:T(8,128)(2,1)S(1)}, u32[]{:S(2)}) copy-start(bf16[8,64,512]{2,1,0:T(8,128)(2,1)S(1)} %bitcast_reduce_fusion) | copy-start | bytes 1572868
  13.2 20.8 %copy-start.8 = (bf16[512,64]{0,1:T(8,128)(2,1)}, bf16[512,64]{0,1:T(8,128)(2,1)S(1)}, u32[]{:S(2)}) copy-start(bf16[512,64]{0,1:T(8,128)(2,1)S(1)} %get-tuple-element.8) | copy-start | bytes 196612
  13.2 146.3 %collective-permute-start = (bf16[31,64,512]{2,1,0:T(8,128)(2,1)}, bf16[31,64,512]{2,1,0:T(8,128)(2,1)}, u32[]{:S(2)}, u32[]{:S(2)}) collective-permute-start(bf16[31,64,512]{2,1,0:T(8,128)(2,1)} %get-tuple-element.7), channel_id=1, source_target_pairs={{0,8},{4,12},{8,16},{12,20},{16,24},{20,28},{1,9},{5,13},{9,17},{1... | collective-permute-start | bytes 6094856 | tf_op jit(solution)/shard_map/ppermute | solution.py:16
  19.4 143.2 %collective-permute-start.1 = (bf16[31,64,512]{2,1,0:T(8,128)(2,1)}, bf16[31,64,512]{2,1,0:T(8,128)(2,1)}, u32[]{:S(2)}, u32[]{:S(2)}) collective-permute-start(bf16[31,64,512]{2,1,0:T(8,128)(2,1)} %get-tuple-element.7), channel_id=1, source_target_pairs={{0,4},{4,8},{8,12},{12,16},{16,20},{20,24},{24,28},{1,5},{5,9},{9,... | collective-permute-start | bytes 6094856 | tf_op jit(solution)/shard_map/ppermute | solution.py:16
  22.1 148.1 %collective-permute-start.2 = (bf16[31,64,512]{2,1,0:T(8,128)(2,1)}, bf16[31,64,512]{2,1,0:T(8,128)(2,1)}, u32[]{:S(2)}, u32[]{:S(2)}) collective-permute-start(bf16[31,64,512]{2,1,0:T(8,128)(2,1)} %get-tuple-element.7), channel_id=1, source_target_pairs={{4,0},{8,4},{12,8},{16,12},{20,16},{24,20},{28,24},{5,1},{9,5},{13... | collective-permute-start | bytes 6094856 | tf_op jit(solution)/shard_map/ppermute | solution.py:16
  23.4 148.1 %collective-permute-start.3 = (bf16[31,64,512]{2,1,0:T(8,128)(2,1)}, bf16[31,64,512]{2,1,0:T(8,128)(2,1)}, u32[]{:S(2)}, u32[]{:S(2)}) collective-permute-start(bf16[31,64,512]{2,1,0:T(8,128)(2,1)} %get-tuple-element.7), channel_id=1, source_target_pairs={{8,0},{12,4},{16,8},{20,12},{24,16},{28,20},{9,1},{13,5},{17,9},{2... | collective-permute-start | bytes 6094856 | tf_op jit(solution)/shard_map/ppermute | solution.py:16
  26.7 89.1 %collective-permute-start.4 = (f32[64,512]{1,0:T(8,128)}, f32[64,512]{1,0:T(8,128)}, u32[]{:S(2)}, u32[]{:S(2)}) collective-permute-start(f32[64,512]{1,0:T(8,128)} %fusion.52), channel_id=1, source_target_pairs={{0,4},{4,0},{8,12},{12,8},{16,20},{20,16},{24,28},{28,24},{1,5},{5... | collective-permute-start | bytes 393224 | tf_op jit(solution)/shard_map/ppermute | solution.py:22
  34.0 1.5 slice-start.1
  37.1 9.9 %slice-start = ((bf16[1023,4096]{1,0:T(8,128)(2,1)}), bf16[192,4096]{1,0:T(8,128)(2,1)S(1)}, s32[]{:S(2)}) async-start(bf16[1023,4096]{1,0:T(8,128)(2,1)} %param.11), calls=%async_computation | async-start | bytes 3145728 | tf_op jit(solution)/shard_map/slice | solution.py:84
  37.1 9.9 %copy-start.11 = (s32[8,24]{1,0:T(8,128)S(1)}, s32[8,24]{1,0:T(8,128)}, u32[]{:S(2)}) copy-start(s32[8,24]{1,0:T(8,128)} %sub.71) | copy-start | bytes 2308
  111.7 2.4 %slice-start.2 = ((bf16[1023,4096]{1,0:T(8,128)(2,1)}), bf16[12,4096]{1,0:T(8,128)(2,1)S(1)}, s32[]{:S(2)}) async-start(bf16[1023,4096]{1,0:T(8,128)(2,1)} %param.11), calls=%async_computation.2 | async-start | bytes 262144 | tf_op jit(solution)/shard_map/slice | solution.py:84
  117.0 36.6 %collective-permute-start.5 = (f32[64,512]{1,0:T(8,128)S(1)}, f32[64,512]{1,0:T(8,128)S(1)}, u32[]{:S(2)}, u32[]{:S(2)}) collective-permute-start(f32[64,512]{1,0:T(8,128)S(1)} %fusion.53), channel_id=1, source_target_pairs={{0,8},{4,12},{8,0},{12,4},{16,24},{20,28},{24,16},{28,20},{1,9},{5... | collective-permute-start | bytes 393224 | tf_op jit(solution)/shard_map/ppermute | solution.py:22
  153.8 5.0 %collective-permute-start.6 = (f32[64,512]{1,0:T(8,128)S(1)}, f32[64,512]{1,0:T(8,128)S(1)}, u32[]{:S(2)}, u32[]{:S(2)}) collective-permute-start(f32[64,512]{1,0:T(8,128)S(1)} %fusion.54), channel_id=1, source_target_pairs={{0,16},{4,20},{8,24},{12,28},{16,0},{20,4},{24,8},{28,12},{1,17},{... | collective-permute-start | bytes 393224 | tf_op jit(solution)/shard_map/ppermute | solution.py:22
  160.4 5.2 %copy-start.5 = (bf16[8,64,512]{2,1,0:T(8,128)(2,1)S(1)}, bf16[8,64,512]{2,1,0:T(8,128)(2,1)}, u32[]{:S(2)}) copy-start(bf16[8,64,512]{2,1,0:T(8,128)(2,1)} %copy-done.4) | copy-start | bytes 1572868
  165.6 2.7 %copy-start.3 = (bf16[16,64,512]{2,1,0:T(8,128)(2,1)S(1)}, bf16[16,64,512]{2,1,0:T(8,128)(2,1)}, u32[]{:S(2)}) copy-start(bf16[16,64,512]{2,1,0:T(8,128)(2,1)} %copy-done.2) | copy-start | bytes 3145732
  167.0 3.1 %copy-start.9 = (bf16[512,64]{0,1:T(8,128)(2,1)S(1)}, bf16[512,64]{0,1:T(8,128)(2,1)}, u32[]{:S(2)}) copy-start(bf16[512,64]{0,1:T(8,128)(2,1)} %copy-done.8) | copy-start | bytes 196612
  171.5 13.9 %slice-start.3 = ((s8[5242880]{0:T(1024)(128)(4,1)}), s8[4194304]{0:T(1024)(128)(4,1)S(1)}, s32[]{:S(2)}) async-start(s8[5242880]{0:T(1024)(128)(4,1)} %bitcast.136), calls=%async_computation.3 | async-start | bytes 8388608
  172.9 12.4 %slice-start.4 = ((s8[5242880]{0:T(1024)(128)(4,1)}), s8[1048576]{0:T(1024)(128)(4,1)S(1)}, s32[]{:S(2)}) async-start(s8[5242880]{0:T(1024)(128)(4,1)} %bitcast.136), calls=%async_computation.4 | async-start | bytes 2097152
  187.9 3.5 %copy-start.7 = (bf16[2,10,64,64]{3,2,1,0:T(8,128)(2,1)S(1)}, bf16[2,10,64,64]{3,2,1,0:T(8,128)(2,1)}, u32[]{:S(2)}) copy-start(bf16[2,10,64,64]{3,2,1,0:T(8,128)(2,1)} %reshape.174) | copy-start | bytes 491524
  187.9 7.0 %copy-start.1 = (bf16[16,64,256]{2,1,0:T(8,128)(2,1)S(1)}, bf16[16,64,256]{2,1,0:T(8,128)(2,1)}, u32[]{:S(2)}) copy-start(bf16[16,64,256]{2,1,0:T(8,128)(2,1)} %param.7) | copy-start | bytes 1572868
  189.0 4.4 %copy-start.10 = (bf16[5,64,64]{2,1,0:T(8,128)(2,1)S(1)}, bf16[5,64,64]{2,1,0:T(8,128)(2,1)}, u32[]{:S(2)}) copy-start(bf16[5,64,64]{2,1,0:T(8,128)(2,1)} %reshape.159) | copy-start | bytes 122884
  193.6 1.3 copy-start.14
  (4 other events, 3.7 us)
where the time goes:
time: 197 us; the launch traced here: 195 us
  local copies, waits for them, and re-layouts  105 us (53%)
  waiting for transfers between devices  36.5 us (19%)
  matrix products  33.8 us (17%)
  starting transfers between devices  15.1 us (8%)
  other arithmetic  3.33 us (2%)
    reshape x5, local copies, waits for them, and re-layouts, couple_level(): dense = placed.astype(jnp.bfloat16).reshape(number, 5 * number, RANK, RANK)  64.8 us
    ppermute x3, waiting for transfers between devices, partner(): return lax.ppermute(value, axis, pairs)  36.5 us
    unnamed x57, local copies, waits for them, and re-layouts  21 us
    dot_general x5, matrix products, couple_level(): jnp.einsum('tks,tkm->tsm', selector, tiles, preferred_element_type=jnp.fl...  13.9 us
    dot_general x5, matrix products, couple_level(): jnp.einsum('tsab,sap->tbp', dense, window, preferred_element_type=jnp.flo...  12.8 us
    ppermute x4, starting transfers between devices, from_behind(): return lax.ppermute(block, axis, route)  11.5 us
    slice x7, local copies, waits for them, and re-layouts, shards(): couplings[cursor:cursor + entries]  6.2 us
    concatenate x5, local copies, waits for them, and re-layouts, shards(): jnp.concatenate([piece[cursor:cursor + number] for piece in received], ax...  5.32 us
  transfers between devices with their start and end apart: 7, of which 2 were waited for; matrix products, arithmetic and copies ran while one was open for 54% of the time, Pallas kernels for 0%

commit v1 on v0

v1 whole, which is shorter than its diff:
```python
import functools

import jax
import jax.numpy as jnp
from jax import lax
from jax.experimental import pallas as pl
from jax.experimental.pallas import tpu as pltpu
from jax.sharding import PartitionSpec as P

RANK = 64
CHUNKS = 4
BF = jnp.bfloat16
F32 = jnp.float32


def matmul(a, b):
    return lax.dot_general(a, b, (((1,), (0,)), ((), ())), preferred_element_type=F32)


def matmul_t(a, b):
    return lax.dot_general(a, b, (((0,), (0,)), ((), ())), preferred_element_type=F32)


class Route:
    def __init__(self, sends, target, takes, origin, after):
        self.sends = sends
        self.target = target
        self.takes = takes
        self.origin = origin
        self.after = after


def routes_of(n, me):
    def among(*devices):
        found = me == devices[0]
        for device in devices[1:]:
            found = found | (me == device)
        return found

    if n == 8:
        flip = [me + 1 - 2 * (me % 2), me + 2 - 4 * ((me // 2) % 2), me + 4 - 8 * (me // 4)]
        other = 7 - me
        always = me >= 0
        cross3 = flip[1] + 1 - 2 * (flip[1] % 2)
        cross6 = flip[1] + 4 - 8 * (flip[1] // 4)
        return [
            Route(always, flip[0], always, flip[0], None),
            Route(always, flip[1], always, flip[1], None),
            Route(among(0, 3, 4, 7), flip[0], among(1, 2, 5, 6), cross3, 1),
            Route(among(0, 1, 6, 7), flip[2], among(2, 3, 4, 5), cross6, 1),
            Route(among(2, 5), flip[0], among(3, 4), other, 3),
        ]
    return [
        Route((me + o >= 0) & (me + o < n), me + o, (me - o >= 0) & (me - o < n), me - o, None)
        for o in (1, -1, 2, -2)
    ]


def kernel(n, leaves, probes, points, basis, lifts, tops, keys, couplings, coupled, ancestors,
           pts, tiles, own, got, got_lifts, lifted, spread, w0, w1, wu, acc, ladder,
           pts_sem, tile_sem, send_sem, recv_sem, up_send, up_recv):
    me = lax.axis_index("leaf")
    ups = n.bit_length() - 1
    leaf = pts.shape[0] // leaves
    per = leaves // CHUNKS
    routes = routes_of(n, me)
    partners = []
    for h in range(ups):
        bit = (me // (1 << h)) % 2
        partners.append((bit, me + (1 << h) * (1 - 2 * bit)))

    def point_copy(k):
        rows = pl.ds(k * per * leaf, per * leaf)
        return pltpu.make_async_copy(points.at[rows, :], pts.at[rows, :], pts_sem.at[k])

    tile_copy = pltpu.make_async_copy(couplings, tiles, tile_sem)
    for k in range(CHUNKS):
        point_copy(k).start()
    tile_copy.start()

    barrier = pltpu.get_barrier_semaphore()
    greeted = [(None, device) for _, device in partners]
    if n != 8:
        greeted += [(r.sends, r.target) for r in routes]
    for valid, device in greeted:
        def greet(device=device):
            pl.semaphore_signal(barrier, inc=1, device_id={"leaf": device},
                                device_id_type=pl.DeviceIdType.MESH)
        greet() if valid is None else pl.when(valid)(greet)
    expected = ups
    if n != 8:
        expected += sum(r.takes.astype(jnp.int32) for r in routes)
    pl.semaphore_wait(barrier, expected)

    def move(i, k):
        route = routes[i]
        if k == CHUNKS:
            src = lifts if route.after is None else got_lifts.at[route.after]
            dst = got_lifts.at[i]
        else:
            rows = pl.ds(k * per * RANK, per * RANK)
            src = own.at[rows, :] if route.after is None else got.at[route.after, rows, :]
            dst = got.at[i, rows, :]
        return pltpu.make_async_remote_copy(
            src_ref=src, dst_ref=dst, send_sem=send_sem.at[i, k], recv_sem=recv_sem.at[i, k],
            device_id={"leaf": route.target}, device_id_type=pl.DeviceIdType.MESH)

    def send(i, k):
        pl.when(routes[i].sends)(lambda: move(i, k).start())

    arrived = set()

    def arrive(i, k):
        if (i, k) in arrived:
            return
        arrived.add((i, k))
        pl.when(routes[i].takes)(lambda: move(i, k).wait_recv())
        for later, route in enumerate(routes):
            if route.after == i:
                send(later, k)

    for i, route in enumerate(routes):
        if route.after is None:
            send(i, CHUNKS)

    for k in range(CHUNKS):
        point_copy(k).wait()
        for j in range(k * per, (k + 1) * per):
            own[j * RANK:(j + 1) * RANK, :] = matmul(
                basis[j], pts[j * leaf:(j + 1) * leaf, :]).astype(BF)
        for i, route in enumerate(routes):
            if route.after is None:
                send(i, k)

    def lift_all(source, matrices):
        half = leaves // 2
        for i in range(leaves - 1):
            if i < half:
                pair = source[2 * i * RANK:(2 * i + 2) * RANK, :]
            else:
                at = 2 * (i - half)
                pair = lifted[at * RANK:(at + 2) * RANK, :]
            lifted[i * RANK:(i + 1) * RANK, :] = matmul(
                matrices[i * RANK:(i + 1) * RANK, :], pair).astype(BF)

    def climb(h):
        bit, device = partners[h]
        return pltpu.make_async_remote_copy(
            src_ref=ladder.at[h, bit], dst_ref=ladder.at[h, bit], send_sem=up_send.at[h],
            recv_sem=up_recv.at[h], device_id={"leaf": device}, device_id_type=pl.DeviceIdType.MESH)

    def climb_end(h):
        climb(h).wait_recv()
        pairs = sum(n >> (g + 1) for g in range(h))
        row = (pairs + me // (1 << (h + 1))) * RANK
        matrix = tops[pl.ds(pl.multiple_of(row, RANK), RANK), :]
        both = ladder[h].reshape(2 * RANK, probes)
        value = matmul(matrix, both).astype(BF)
        ancestors[0, h] = value
        if h + 1 < ups:
            ladder[h + 1, partners[h + 1][0]] = value
            climb(h + 1).start()

    lift_all(own, lifts)
    ladder[0, partners[0][0]] = lifted[(leaves - 2) * RANK:(leaves - 1) * RANK, :]
    climb(0).start()

    tile_copy.wait()
    wide = 512

    def two_sides(block, first_half):
        block = block.astype(F32)
        rolled = jnp.concatenate(
            [pltpu.roll(block[:, g * 128:(g + 1) * 128], 64, 1) for g in range(wide // 128)], axis=1)
        lane = lax.broadcasted_iota(jnp.int32, block.shape, 1) % 128 < 64
        keep = lane == first_half
        even = jnp.where(keep, jnp.where(first_half, block, rolled), 0.0)
        odd = jnp.where(keep, jnp.where(first_half, rolled, block), 0.0)
        return even.astype(BF), odd.astype(BF)

    def one_hot(row, count, entries, allowed=None):
        slots = lax.broadcasted_iota(jnp.int32, (count, entries), 0)
        hit = slots == keys[row:row + 1, :entries] if isinstance(row, int) else (
            slots == keys[pl.ds(row, 1), :][:, :entries])
        if allowed is not None:
            hit = hit & allowed
        return jnp.where(hit, 1.0, 0.0).astype(BF)

    def put(evens, odds, base, ref_of, group, lanes):
        both = jnp.concatenate([evens[base:base + 8], odds[base:base + 8]], axis=0).astype(BF)
        for q in range(wide // 128):
            at = (group * (wide // 128) + q) * 16
            ref_of[at:at + 16, lanes] = both[:, q * 128:(q + 1) * 128]

    groups = RANK * RANK // wide
    e0, e1 = 6 * leaves, 3 * leaves

    def place0(j):
        rows = pl.ds(pl.multiple_of(j * e0, 32), e0)
        lanes = pl.ds(pl.multiple_of(j * 128, 128), 128)
        first = lax.broadcasted_iota(jnp.int32, (e0, wide), 0) < e0 // 2
        hot = one_hot(j, 5 * leaves, e0)
        for g in range(groups):
            even, odd = two_sides(tiles[rows, g * wide:(g + 1) * wide], first)
            evens, odds = matmul(hot, even), matmul(hot, odd)
            for d in range(5):
                for half in range(2):
                    put(evens, odds, d * leaves + half * 8, w0.at[d, half], g, lanes)

    def place1(j):
        rows = pl.ds(pl.multiple_of(leaves * e1 + j * e1, 16), e1)
        lanes = pl.ds(pl.multiple_of(j * 128, 128), 128)
        first = lax.broadcasted_iota(jnp.int32, (e1, wide), 0) < e1 // 2
        hot = one_hot(leaves // 2 + j, 5 * 8, e1)
        for g in range(groups):
            even, odd = two_sides(tiles[rows, g * wide:(g + 1) * wide], first)
            evens, odds = matmul(hot, even), matmul(hot, odd)
            for d in range(5):
                put(evens, odds, d * 8, w1.at[d], g, lanes)

    def place_upper():
        start = leaves * e1 + (leaves // 2) * (e1 // 2)
        count = tiles.shape[0] - start
        row = lax.broadcasted_iota(jnp.int32, (count, wide), 0)
        first = (row < 12) | ((row >= 24) & (row < 36)) | ((row >= 48) & (row < 54)) | (row >= 60)
        entry = lax.broadcasted_iota(jnp.int32, (40, count), 1)
        hots = []
        for low, high in ((0, 24), (24, 48), (48, 60), (60, 63)):
            hots.append(one_hot(3 * leaves // 4, 40, count, (entry >= low) & (entry < high)))
        hot = jnp.concatenate(hots, axis=0)
        for g in range(groups):
            even, odd = two_sides(tiles[start:, g * wide:(g + 1) * wide], first)
            evens, odds = matmul(hot, even), matmul(hot, odd)
            for j in range(4):
                for d in range(5):
                    put(evens, odds, j * 40 + d * 8, wu.at[d], g, slice(j * 128, (j + 1) * 128))

    def spread_rows(source, first, blocks):
        for s, block in enumerate(blocks):
            at = (first + block) * RANK
            rows = source[at:at + RANK, :].astype(F32)
            for c in range(probes // 128):
                spread[c, pl.ds(s, RANK, stride=8), :] = rows[:, c * 128:(c + 1) * 128]
        return jnp.concatenate([spread[c].astype(BF) for c in range(probes // 128)], axis=1)

    def add_in(weights, columns, base, moments, fresh):
        @pl.loop(0, columns // 256)
        def _(c):
            at = pl.multiple_of(c * 256, 256)
            part = matmul_t(weights[:, pl.ds(at, 256)], moments)
            rows = pl.ds(pl.multiple_of(base + at, 256), 256)
            if fresh:
                acc[rows, :] = part
            else:
                acc[rows, :] += part

    def couple(source, matrices, d, fresh=False, lift=True):
        if lift:
            lift_all(source, matrices)
        width = leaves * RANK
        add_in(w0.at[d, 0], width, 0, spread_rows(source, 0, range(8)), fresh)
        add_in(w0.at[d, 1], width, 0, spread_rows(source, 8, range(8)), False)
        add_in(w1.at[d], width // 2, width, spread_rows(lifted, 0, range(8)), fresh)
        add_in(wu.at[d], width // 2, width + width // 2,
               spread_rows(lifted, 8, (0, 1, 2, 3, 4, 5, 6, 6)), fresh)

    passed_on = sorted({r.after for r in routes if r.after is not None})
    for i in passed_on:
        arrive(i, CHUNKS)
    for step in range(4):
        @pl.loop(2 * step, 2 * step + 2)
        def _(j):
            place0(j)
        if step < CHUNKS - 1:
            for i in passed_on:
                arrive(i, step)
        if step < ups:
            climb_end(step)
    for h in range(4, ups):
        climb_end(h)
    pl.loop(0, leaves // 4)(place1)
    place_upper()
    for i in passed_on:
        arrive(i, CHUNKS - 1)
    couple(own, lifts, 2, fresh=True, lift=False)
    for i, route in enumerate(routes):
        for k in range(CHUNKS + 1):
            arrive(i, k)

        @pl.when(route.takes)
        def _():
            couple(got.at[i], got_lifts.at[i], route.origin - me + 2)

    for t in range(2 * leaves - 1):
        coupled[t] = acc[t * RANK:(t + 1) * RANK, :].astype(BF)

    for i, route in enumerate(routes):
        for k in range(CHUNKS + 1):
            pl.when(route.sends)(lambda i=i, k=k: move(i, k).wait_send())
    for h in range(ups):
        climb(h).wait_send()


def side_by_side(matrices):
    pairs = matrices.reshape(-1, 2, RANK, RANK).transpose(0, 3, 1, 2)
    return pairs.reshape(-1, 2 * RANK)


def source_keys(sources, device, leaves):
    rows, cursor = [], 0
    upper = []
    for height in range(leaves.bit_length()):
        number = leaves >> height
        entries = 3 * number * number
        local = sources[cursor:cursor + entries] - (device - 2) * number
        cursor += entries
        if height < 2:
            local = local.reshape(number // 2, 6 * number)
            rows.append(jnp.pad(local, ((0, 0), (0, 128 - 6 * number)), constant_values=-1))
        else:
            shift = 8 - 2 * number
            upper.append(local // number * 8 + local % number + shift)
    last = jnp.concatenate(upper)
    rows.append(jnp.pad(last, (0, 128 - last.shape[0]), constant_values=-1)[None])
    rows.append(jnp.full((3, 128), -1, jnp.int32))
    return jnp.concatenate(rows, axis=0)


def shards(points, leaf_basis, local_transfer, top_transfer, sources, couplings):
    n = lax.axis_size("leaf")
    leaves, _, leaf = leaf_basis.shape
    probes = points.shape[1]
    ups = n.bit_length() - 1
    keys = source_keys(sources, lax.axis_index("leaf"), leaves)
    block = leaves * RANK
    count = 5 if n == 8 else 4
    vmem = pl.BlockSpec(memory_space=pltpu.VMEM)
    anywhere = pl.BlockSpec(memory_space=pl.ANY)
    return pl.pallas_call(
        functools.partial(kernel, n, leaves, probes),
        out_shape=(
            jax.ShapeDtypeStruct((2 * leaves - 1, RANK, probes), BF),
            jax.ShapeDtypeStruct((1, ups, RANK, probes), BF),
        ),
        in_specs=[anywhere, vmem, vmem, vmem, vmem, anywhere],
        out_specs=(vmem, vmem),
        scratch_shapes=[
            pltpu.VMEM(points.shape, BF),
            pltpu.VMEM(couplings.shape, BF),
            pltpu.VMEM((block, probes), BF),
            pltpu.VMEM((count, block, probes), BF),
            pltpu.VMEM((count, block - RANK, 2 * RANK), BF),
            pltpu.VMEM((block - RANK, probes), BF),
            pltpu.VMEM((probes // 128, 8 * RANK, 128), F32),
            pltpu.VMEM((5, 2, 8 * RANK, block), BF),
            pltpu.VMEM((5, 8 * RANK, block // 2), BF),
            pltpu.VMEM((5, 8 * RANK, block // 2), BF),
            pltpu.VMEM((2 * block, probes), F32),
            pltpu.VMEM((ups, 2, RANK, probes), BF),
            pltpu.SemaphoreType.DMA((CHUNKS,)),
            pltpu.SemaphoreType.DMA,
            pltpu.SemaphoreType.DMA((count, CHUNKS + 1)),
            pltpu.SemaphoreType.DMA((count, CHUNKS + 1)),
            pltpu.SemaphoreType.DMA((ups,)),
            pltpu.SemaphoreType.DMA((ups,)),
        ],
        compiler_params=pltpu.CompilerParams(
            collective_id=0, has_side_effects=True, vmem_limit_bytes=60 * 2**20),
    )(points, leaf_basis, side_by_side(local_transfer), side_by_side(top_transfer), keys, couplings)


def solution(mesh):
    placed = (
        P("leaf", "probe"),
        P("leaf", None, None),
        P("leaf", None),
        P(),
        P("leaf"),
        P("leaf", None),
    )
    return jax.shard_map(
        shards,
        mesh=mesh,
        in_specs=placed,
        out_specs=(P("leaf", None, "probe"), P("leaf", None, None, "probe")),
        check_vma=False,
    )
```

time: 197 us -> 93.4 us (0.47)
  the two profiles are of different devices: /device:TPU:0 before, /device:TPU:26 now
where the time goes in v1:
time: 93.4 us; the launch traced here: 93 us
  Pallas kernels  78.3 us (84%)
  local copies, waits for them, and re-layouts  9.59 us (10%)
  other arithmetic  4.43 us (5%)
    pallas_call x1, Pallas kernels, shards(): pl.pallas_call(functools.partial(kernel, n, leaves, probes), out_shape=(j...  78.3 us
    reshape x4, local copies, waits for them, and re-layouts, side_by_side(): pairs = matrices.reshape(-1, 2, RANK, RANK).transpose(0, 3, 1, 2)  3.83 us
    unnamed x4, local copies, waits for them, and re-layouts  3.79 us
    add x3, other arithmetic, source_keys(): upper.append(local // number * 8 + local % number + shift)  2.3 us

profile of v1, /device:TPU:26, one launch (start us, length us, event | category | flops | bytes accessed | tf_op | source)
XLA Modules:
  0.0 93.0 jit_solution(3613686780539246465)
XLA Ops:
  0.6 0.8 fusion.3
  1.4 0.8 multiply_add_fusion
  2.2 0.8 fusion.5
  2.9 0.1 pad_add_fusion
  3.0 0.7 slice_subtract_fusion.1
  3.7 0.1 pad.18.clone
  3.8 0.1 sub.63
  3.9 0.7 slice_subtract_fusion
  4.6 0.1 sub.60
  4.6 0.7 fusion.1.keys
  5.3 1.1 %reshape.26 = bf16[7,2,64,64]{3,2,1,0:T(8,128)(2,1)S(1)} reshape(bf16[14,4096]{1,0:T(8,128)(2,1)} %param.9) | data formatting | bytes 229376 | tf_op jit(solution)/shard_map/reshape | solution.py:305
  6.5 0.2 copy.9
  6.6 0.8 reshape.27.tops
  7.4 1.4 %reshape.24 = bf16[15,2,64,64]{3,2,1,0:T(8,128)(2,1)S(1)} reshape(bf16[30,4096]{1,0:T(8,128)(2,1)} %param.8) | data formatting | bytes 491520 | tf_op jit(solution)/shard_map/reshape | solution.py:305
  8.9 1.1 %copy.8 = bf16[15,2,64,64]{2,1,3,0:T(2,128)(2,1)S(1)} copy(bf16[15,2,64,64]{3,2,1,0:T(8,128)(2,1)S(1)} %reshape.24) | data formatting | bytes 491520 | tf_op jit(solution)/shard_map/reshape | solution.py:305
  10.0 0.9 %reshape.25.lifts = bf16[960,128]{1,0:T(8,128)(2,1)} reshape(bf16[15,64,2,64]{3,2,1,0:T(2,128)(2,1)S(1)} %bitcast.4) | data formatting | bytes 491520 | tf_op jit(solution)/shard_map/reshape | solution.py:306
  10.9 78.3 %shard_map.77 = (bf16[31,64,512]{2,1,0:T(8,128)(2,1)}, bf16[1,3,64,512]{3,2,1,0:T(8,128)(2,1)}) custom-call(bf16[4096,512]{1,0:T(8,128)(2,1)} %points.1, bf16[16,64,256]{2,1,0:T(8,128)(2,1)} %basis.1, bf16[960,128]{1,0:T(8,128)(2,1)} %reshape.25.lifts, bf16[448,128]{1,0:T(8,128)(2,1)} %reshape.27.tops, s32[16,128]{1,0:T(8,128)} %fusion.1.keys, ...), custom_call_target="tpu_custom_call" | custom-call | tf_op jit(solution)/shard_map/pallas_call | solution.py:339
  89.2 0.0 copy-start
  89.2 3.1 %copy.12 = bf16[31,64,512]{2,1,0:T(8,128)(2,1)} copy(bf16[31,64,512]{2,1,0:T(8,128)(2,1)} %get-tuple-element.4) | data formatting | bytes 4063232
  92.3 0.0 copy-done
  92.3 0.7 copy.13
  (2 shorter events, 0.0 us)
Async XLA Ops:
  89.2 3.1 %copy-start = (bf16[1,3,64,512]{3,2,1,0:T(8,128)(2,1)S(1)}, bf16[1,3,64,512]{3,2,1,0:T(8,128)(2,1)}, u32[]{:S(2)}) copy-start(bf16[1,3,64,512]{3,2,1,0:T(8,128)(2,1)} %get-tuple-element.5) | copy-start | bytes 589828

commit v2 on v1

--- a/solution.py
+++ b/solution.py
@@ -2,6 +2,7 @@
 
 import jax
 import jax.numpy as jnp
+import numpy as np
 from jax import lax
 from jax.experimental import pallas as pl
 from jax.experimental.pallas import tpu as pltpu
@@ -56,8 +57,9 @@
     ]
 
 
-def kernel(n, leaves, probes, points, basis, lifts, tops, keys, couplings, coupled, ancestors,
-           pts, tiles, own, got, got_lifts, lifted, spread, w0, w1, wu, acc, ladder,
+def kernel(n, leaves, probes, points, basis, lifts, tops, holders, couplings, coupled, ancestors,
+           pts, tiles, own, got, got_lifts, lifted, spread, unrolled, square, w0, w1, wu, acc,
+           ladder,
            pts_sem, tile_sem, send_sem, recv_sem, up_send, up_recv):
     me = lax.axis_index("leaf")
     ups = n.bit_length() - 1
@@ -162,115 +164,96 @@
             climb(h + 1).start()
 
     lift_all(own, lifts)
-    ladder[0, partners[0][0]] = lifted[(leaves - 2) * RANK:(leaves - 1) * RANK, :]
+    root = lifted[(leaves - 2) * RANK:(leaves - 1) * RANK, :].astype(F32)
+    for c in range(probes // 128):
+        for side in range(2):
+            spread[c, pl.ds(side, RANK // 2, stride=2), :] = root[
+                side * 32:(side + 1) * 32, c * 128:(c + 1) * 128]
+    ladder[0, partners[0][0]] = jnp.concatenate(
+        [spread[c] for c in range(probes // 128)], axis=1).astype(BF)
     climb(0).start()
 
     tile_copy.wait()
-    wide = 512
-
-    def two_sides(block, first_half):
-        block = block.astype(F32)
-        rolled = jnp.concatenate(
-            [pltpu.roll(block[:, g * 128:(g + 1) * 128], 64, 1) for g in range(wide // 128)], axis=1)
-        lane = lax.broadcasted_iota(jnp.int32, block.shape, 1) % 128 < 64
-        keep = lane == first_half
-        even = jnp.where(keep, jnp.where(first_half, block, rolled), 0.0)
-        odd = jnp.where(keep, jnp.where(first_half, rolled, block), 0.0)
-        return even.astype(BF), odd.astype(BF)
-
-    def one_hot(row, count, entries, allowed=None):
-        slots = lax.broadcasted_iota(jnp.int32, (count, entries), 0)
-        hit = slots == keys[row:row + 1, :entries] if isinstance(row, int) else (
-            slots == keys[pl.ds(row, 1), :][:, :entries])
-        if allowed is not None:
-            hit = hit & allowed
-        return jnp.where(hit, 1.0, 0.0).astype(BF)
-
-    def put(evens, odds, base, ref_of, group, lanes):
-        both = jnp.concatenate([evens[base:base + 8], odds[base:base + 8]], axis=0).astype(BF)
-        for q in range(wide // 128):
-            at = (group * (wide // 128) + q) * 16
-            ref_of[at:at + 16, lanes] = both[:, q * 128:(q + 1) * 128]
-
-    groups = RANK * RANK // wide
+    square[0] = jnp.zeros((32, 128), BF)
+
+    def open_rows(start, count, turn):
+        for q in range(32):
+            part = tiles[pl.ds(start, count), q * 128:(q + 1) * 128].astype(F32)
+            unrolled[pl.ds(q, count, stride=32), :] = turn(part)
+        square[pl.ds(start + 1, count)] = unrolled[:count * 32, :].astype(BF).reshape(count, 32, 128)
+
+    def open_group(group, turns):
+        def turn(part):
+            return jnp.concatenate(
+                [pltpu.roll(part[u * 8:(u + 1) * 8], turns[u], 1) for u in range(2)], axis=0)
+        open_rows(pl.multiple_of(group * 16, 16), 16, turn)
+
     e0, e1 = 6 * leaves, 3 * leaves
 
-    def place0(j):
-        rows = pl.ds(pl.multiple_of(j * e0, 32), e0)
-        lanes = pl.ds(pl.multiple_of(j * 128, 128), 128)
-        first = lax.broadcasted_iota(jnp.int32, (e0, wide), 0) < e0 // 2
-        hot = one_hot(j, 5 * leaves, e0)
-        for g in range(groups):
-            even, odd = two_sides(tiles[rows, g * wide:(g + 1) * wide], first)
-            evens, odds = matmul(hot, even), matmul(hot, odd)
-            for d in range(5):
-                for half in range(2):
-                    put(evens, odds, d * leaves + half * 8, w0.at[d, half], g, lanes)
-
-    def place1(j):
-        rows = pl.ds(pl.multiple_of(leaves * e1 + j * e1, 16), e1)
-        lanes = pl.ds(pl.multiple_of(j * 128, 128), 128)
-        first = lax.broadcasted_iota(jnp.int32, (e1, wide), 0) < e1 // 2
-        hot = one_hot(leaves // 2 + j, 5 * 8, e1)
-        for g in range(groups):
-            even, odd = two_sides(tiles[rows, g * wide:(g + 1) * wide], first)
-            evens, odds = matmul(hot, even), matmul(hot, odd)
-            for d in range(5):
-                put(evens, odds, d * 8, w1.at[d], g, lanes)
-
-    def place_upper():
+    def open0(group):
+        amount = (group // 3) % 2 * 64
+        open_group(group, (amount, amount))
+
+    def open1(step):
+        open_group(step + leaves * 3 * leaves // 16,
+                   ((2 * step // 3) % 2 * 64, ((2 * step + 1) // 3) % 2 * 64))
+
+    def open_upper():
         start = leaves * e1 + (leaves // 2) * (e1 // 2)
-        count = tiles.shape[0] - start
-        row = lax.broadcasted_iota(jnp.int32, (count, wide), 0)
-        first = (row < 12) | ((row >= 24) & (row < 36)) | ((row >= 48) & (row < 54)) | (row >= 60)
-        entry = lax.broadcasted_iota(jnp.int32, (40, count), 1)
-        hots = []
-        for low, high in ((0, 24), (24, 48), (48, 60), (60, 63)):
-            hots.append(one_hot(3 * leaves // 4, 40, count, (entry >= low) & (entry < high)))
-        hot = jnp.concatenate(hots, axis=0)
-        for g in range(groups):
-            even, odd = two_sides(tiles[start:, g * wide:(g + 1) * wide], first)
-            evens, odds = matmul(hot, even), matmul(hot, odd)
-            for j in range(4):
-                for d in range(5):
-                    put(evens, odds, j * 40 + d * 8, wu.at[d], g, slice(j * 128, (j + 1) * 128))
-
-    def spread_rows(source, first, blocks):
-        for s, block in enumerate(blocks):
-            at = (first + block) * RANK
-            rows = source[at:at + RANK, :].astype(F32)
-            for c in range(probes // 128):
-                spread[c, pl.ds(s, RANK, stride=8), :] = rows[:, c * 128:(c + 1) * 128]
-        return jnp.concatenate([spread[c].astype(BF) for c in range(probes // 128)], axis=1)
+        for low in range(start, tiles.shape[0], 16):
+            count = min(16, tiles.shape[0] - low)
+            row = lax.broadcasted_iota(jnp.int32, (count, 128), 0) + (low - start)
+            first = ((row < 12) | ((row >= 24) & (row < 36)) | ((row >= 48) & (row < 54))
+                     | (row >= 60))
+            open_rows(low, count, lambda part: jnp.where(first, part, pltpu.roll(part, 64, 1)))
+
+    low_half = jnp.where(lax.broadcasted_iota(jnp.int32, (32, 128), 1) < 64, 1.0, 0.0)
+    low_half = low_half.astype(BF) > BF(0.5)
+
+    def place(weights, base, pair, slots):
+        lanes = pl.ds(pl.multiple_of(pair * 128, 128), 128)
+        for d in range(5):
+            for s in range(slots):
+                at = base + pair * 10 * slots + d * slots + s
+                one = square[holders[at]]
+                two = square[holders[at + 5 * slots]]
+                rows = slice(s * 32, (s + 1) * 32)
+                weights[d, 0, rows, lanes] = jnp.where(low_half, one, two)
+                weights[d, 1, rows, lanes] = jnp.where(low_half, two, one)
+
+    def halves(source, blocks):
+        return [jnp.concatenate([source[s * RANK + side * 32:s * RANK + side * 32 + 32, :]
+                                 for s in blocks], axis=0) for side in range(2)]
 
     def add_in(weights, columns, base, moments, fresh):
-        @pl.loop(0, columns // 256)
+        @pl.loop(0, columns // 512)
         def _(c):
-            at = pl.multiple_of(c * 256, 256)
-            part = matmul_t(weights[:, pl.ds(at, 256)], moments)
-            rows = pl.ds(pl.multiple_of(base + at, 256), 256)
-            if fresh:
-                acc[rows, :] = part
-            else:
-                acc[rows, :] += part
+            at = pl.multiple_of(c * 512, 512)
+            even = matmul_t(weights[0, :, pl.ds(at, 512)], moments[0])
+            odd = matmul_t(weights[1, :, pl.ds(at, 512)], moments[1])
+            for t in range(8):
+                rows = pl.ds(pl.multiple_of(base + at + t * RANK, RANK), RANK)
+                swap = t + 1 - 2 * (t % 2)
+                part = even[t * RANK:(t + 1) * RANK] + odd[swap * RANK:(swap + 1) * RANK]
+                if fresh:
+                    acc[rows, :] = part
+                else:
+                    acc[rows, :] += part
 
     def couple(source, matrices, d, fresh=False, lift=True):
         if lift:
             lift_all(source, matrices)
         width = leaves * RANK
-        add_in(w0.at[d, 0], width, 0, spread_rows(source, 0, range(8)), fresh)
-        add_in(w0.at[d, 1], width, 0, spread_rows(source, 8, range(8)), False)
-        add_in(w1.at[d], width // 2, width, spread_rows(lifted, 0, range(8)), fresh)
+        add_in(w0.at[d], width, 0, halves(source, range(leaves)), fresh)
+        add_in(w1.at[d], width // 2, width, halves(lifted, range(8)), fresh)
         add_in(wu.at[d], width // 2, width + width // 2,
-               spread_rows(lifted, 8, (0, 1, 2, 3, 4, 5, 6, 6)), fresh)
+               halves(lifted, (8, 9, 10, 11, 12, 13, 14, 14)), fresh)
 
     passed_on = sorted({r.after for r in routes if r.after is not None})
     for i in passed_on:
         arrive(i, CHUNKS)
     for step in range(4):
-        @pl.loop(2 * step, 2 * step + 2)
-        def _(j):
-            place0(j)
+        pl.loop(12 * step, 12 * step + 12)(open0)
         if step < CHUNKS - 1:
             for i in passed_on:
                 arrive(i, step)
@@ -278,8 +261,11 @@
             climb_end(step)
     for h in range(4, ups):
         climb_end(h)
-    pl.loop(0, leaves // 4)(place1)
-    place_upper()
+    pl.loop(0, 12)(open1)
+    open_upper()
+    pl.loop(0, 8)(lambda j: place(w0, 0, j, 16))
+    pl.loop(0, 4)(lambda j: place(w1, 1280, j, 8))
+    pl.loop(0, 4)(lambda j: place(wu, 1600, j, 8))
     for i in passed_on:
         arrive(i, CHUNKS - 1)
     couple(own, lifts, 2, fresh=True, lift=False)
@@ -301,29 +287,35 @@
         climb(h).wait_send()
 
 
-def side_by_side(matrices):
-    pairs = matrices.reshape(-1, 2, RANK, RANK).transpose(0, 3, 1, 2)
-    return pairs.reshape(-1, 2 * RANK)
-
-
-def source_keys(sources, device, leaves):
-    rows, cursor = [], 0
-    upper = []
+def side_by_side(matrices, halved):
+    if halved:
+        split = matrices.reshape(-1, 2, RANK // 2, 2, RANK // 2, 2)
+        return split.transpose(0, 5, 4, 1, 3, 2).reshape(-1, 2 * RANK)
+    return matrices.reshape(-1, 2, RANK, RANK).transpose(0, 3, 1, 2).reshape(-1, 2 * RANK)
+
+
+def source_holders(sources, device, leaves):
+    shifts, bases, widths = [], [], []
     for height in range(leaves.bit_length()):
         number = leaves >> height
-        entries = 3 * number * number
-        local = sources[cursor:cursor + entries] - (device - 2) * number
-        cursor += entries
-        if height < 2:
-            local = local.reshape(number // 2, 6 * number)
-            rows.append(jnp.pad(local, ((0, 0), (0, 128 - 6 * number)), constant_values=-1))
+        target = np.repeat(np.arange(number), 3 * number)
+        if height == 0:
+            bases.append(target * 5 * leaves)
+        elif height == 1:
+            bases.append(5 * leaves * leaves + target * 40)
         else:
-            shift = 8 - 2 * number
-            upper.append(local // number * 8 + local % number + shift)
-    last = jnp.concatenate(upper)
-    rows.append(jnp.pad(last, (0, 128 - last.shape[0]), constant_values=-1)[None])
-    rows.append(jnp.full((3, 128), -1, jnp.int32))
-    return jnp.concatenate(rows, axis=0)
+            first = 8 - 2 * number
+            bases.append(5 * leaves * leaves + 320 + (target + first) * 40 + first)
+        shifts.append(np.full(3 * number * number, number.bit_length() - 1))
+        widths.append(np.full(3 * number * number, leaves if height == 0 else 8))
+    shift, base, width = (
+        jnp.asarray(np.concatenate(x), jnp.int32) for x in (shifts, bases, widths))
+    local = sources - ((device - 2) << shift)
+    subtree = local >> shift
+    key = base + subtree * width + local - (subtree << shift)
+    slots = jnp.arange(5 * leaves * leaves + 640, dtype=jnp.int32)
+    entry = jnp.arange(1, sources.shape[0] + 1, dtype=jnp.int32)
+    return jnp.where(key[:, None] == slots[None, :], entry[:, None], 0).sum(axis=0)
 
 
 def shards(points, leaf_basis, local_transfer, top_transfer, sources, couplings):
@@ -331,7 +323,9 @@
     leaves, _, leaf = leaf_basis.shape
     probes = points.shape[1]
     ups = n.bit_length() - 1
-    keys = source_keys(sources, lax.axis_index("leaf"), leaves)
+    holders = source_holders(sources, lax.axis_index("leaf"), leaves)
+    halved_basis = leaf_basis.reshape(leaves, RANK // 2, 2, leaf).swapaxes(1, 2)
+    halved_basis = halved_basis.reshape(leaves, RANK, leaf)
     block = leaves * RANK
     count = 5 if n == 8 else 4
     vmem = pl.BlockSpec(memory_space=pltpu.VMEM)
@@ -342,7 +336,7 @@
             jax.ShapeDtypeStruct((2 * leaves - 1, RANK, probes), BF),
             jax.ShapeDtypeStruct((1, ups, RANK, probes), BF),
         ),
-        in_specs=[anywhere, vmem, vmem, vmem, vmem, anywhere],
+        in_specs=[anywhere, vmem, vmem, vmem, pl.BlockSpec(memory_space=pltpu.SMEM), anywhere],
         out_specs=(vmem, vmem),
         scratch_shapes=[
             pltpu.VMEM(points.shape, BF),
@@ -351,10 +345,12 @@
             pltpu.VMEM((count, block, probes), BF),
             pltpu.VMEM((count, block - RANK, 2 * RANK), BF),
             pltpu.VMEM((block - RANK, probes), BF),
-            pltpu.VMEM((probes // 128, 8 * RANK, 128), F32),
-            pltpu.VMEM((5, 2, 8 * RANK, block), BF),
-            pltpu.VMEM((5, 8 * RANK, block // 2), BF),
-            pltpu.VMEM((5, 8 * RANK, block // 2), BF),
+            pltpu.VMEM((probes // 128, RANK, 128), F32),
+            pltpu.VMEM((16 * 32, 128), F32),
+            pltpu.VMEM((couplings.shape[0] + 1, 32, 128), BF),
+            pltpu.VMEM((5, 2, block // 2, block), BF),
+            pltpu.VMEM((5, 2, block // 4, block // 2), BF),
+            pltpu.VMEM((5, 2, block // 4, block // 2), BF),
             pltpu.VMEM((2 * block, probes), F32),
             pltpu.VMEM((ups, 2, RANK, probes), BF),
             pltpu.SemaphoreType.DMA((CHUNKS,)),
@@ -366,7 +362,8 @@
         ],
         compiler_params=pltpu.CompilerParams(
             collective_id=0, has_side_effects=True, vmem_limit_bytes=60 * 2**20),
-    )(points, leaf_basis, side_by_side(local_transfer), side_by_side(top_transfer), keys, couplings)
+    )(points, halved_basis, side_by_side(local_transfer, True),
+      side_by_side(top_transfer, False), holders, couplings)
 
 
 def solution(mesh):

time: 93.4 us -> 147 us (1.57)
  local copies, waits for them, and re-layouts: 9.59 us -> 72.3 us
  Pallas kernels: 78.3 us -> 71.3 us
  other arithmetic: 4.43 us -> 2.38 us
    reshape x6 -> x7, local copies, waits for them, and re-layouts: 5.56 us -> 39.9 us  [the longest x1 36.4 us: side_by_side(): split = matrices.reshape(-1, 2, RANK // 2, 2, RANK // 2, 2)]
    transpose x0 -> x1, local copies, waits for them, and re-layouts: none -> 27.6 us  [side_by_side(): return split.transpose(0, 5, 4, 1, 3, 2).reshape(-1, 2 * RANK)]
    pallas_call x1, Pallas kernels: 78.3 us -> 71.3 us  [shards(): pl.pallas_call(functools.partial(kernel, n, leaves, probes), out_shape=(j...]
    add x3 -> x0, other arithmetic: 2.3 us -> none  [source_keys(): upper.append(local // number * 8 + local % number + shift)]
    reduce_sum x0 -> x1, other arithmetic: none -> 1.63 us  [source_holders(): jnp.where(key[:, None] == slots[None, :], entry[:, None], 0).sum(axis=0)]
    unnamed x4 -> x6, local copies, waits for them, and re-layouts: 3.79 us -> 4.69 us
where the time goes in v2:
time: 147 us
  local copies, waits for them, and re-layouts  72.3 us (49%)
  Pallas kernels  71.3 us (49%)
  other arithmetic  2.38 us (2%)
    pallas_call x1, Pallas kernels, shards(): pl.pallas_call(functools.partial(kernel, n, leaves, probes), out_shape=(j...  71.3 us
    reshape x1, local copies, waits for them, and re-layouts, side_by_side(): split = matrices.reshape(-1, 2, RANK // 2, 2, RANK // 2, 2)  36.4 us
    transpose x1, local copies, waits for them, and re-layouts, side_by_side(): return split.transpose(0, 5, 4, 1, 3, 2).reshape(-1, 2 * RANK)  27.6 us
    unnamed x6, local copies, waits for them, and re-layouts  4.69 us

profile of v2, /device:TPU:26, one launch (start us, length us, event | category | flops | bytes accessed | tf_op | source)
XLA Modules:
  0.0 146.6 jit_solution(18138192259411134601)
XLA Ops:
  0.6 0.8 fusion
  1.4 1.6 %select_reduce_fusion.holders = s32[1920]{0:T(1024)} fusion(s32[1023]{0:T(1024)S(1)} %get-tuple-element.3, s32[1023]{0:T(1024)S(1)} %get-tuple-element.2), kind=kLoop, calls=%fused_computation | loop fusion | flops 5890560 | bytes 15864 | tf_op jit(solution)/shard_map/reduce_sum | solution.py:318
  3.0 36.4 %reshape.29 = bf16[15,2,32,2,32,2]{5,4,3,2,1,0:T(8,128)(2,1)} reshape(bf16[30,4096]{1,0:T(8,128)(2,1)} %param.11) | data formatting | bytes 491520 | tf_op jit(solution)/shard_map/reshape | solution.py:292
  39.5 0.0 copy-start
  39.5 0.0 copy-start.1
  39.5 27.6 %copy.18 = bf16[15,2,32,2,2,32]{5,4,3,2,1,0:T(2,128)(2,1)S(1)} copy(bf16[15,2,32,2,2,32]{1,2,4,5,3,0:T(8,128)(2,1)} %bitcast.5) | data formatting | bytes 491520 | tf_op jit(solution)/shard_map/transpose | solution.py:293
  67.1 1.2 reshape.30.lifts
  68.3 0.0 copy-done
  68.3 0.2 reshape.27
  68.5 0.9 copy.17
  69.4 0.0 copy-done.1
  69.4 0.2 reshape.31
  69.6 0.2 copy.19
  69.8 0.8 reshape.32.tops
  70.6 71.3 %shard_map.104 = (bf16[31,64,512]{2,1,0:T(8,128)(2,1)}, bf16[1,3,64,512]{3,2,1,0:T(8,128)(2,1)}) custom-call(bf16[4096,512]{1,0:T(8,128)(2,1)} %points.1, bf16[16,64,256]{2,1,0:T(8,128)(2,1)} %bitcast.6, bf16[960,128]{1,0:T(8,128)(2,1)} %reshape.30.lifts, bf16[448,128]{1,0:T(8,128)(2,1)} %reshape.32.tops, s32[1920]{0:T(1024)} %select_reduce_fusion.holders, ...), custom_call_target="tpu_custom_call" | custom-call | tf_op jit(solution)/shard_map/pallas_call | solution.py:333
  141.9 3.1 %copy.22 = bf16[31,64,512]{2,1,0:T(8,128)(2,1)} copy(bf16[31,64,512]{2,1,0:T(8,128)(2,1)} %get-tuple-element.6) | data formatting | bytes 4063232
  145.0 1.6 %copy.23 = bf16[1,3,64,512]{3,2,1,0:T(8,128)(2,1)} copy(bf16[1,3,64,512]{3,2,1,0:T(8,128)(2,1)} %get-tuple-element.7) | data formatting | bytes 393216
Async XLA Ops:
  39.5 28.9 %copy-start = (bf16[16,64,256]{2,1,0:T(8,128)(2,1)S(1)}, bf16[16,64,256]{2,1,0:T(8,128)(2,1)}, u32[]{:S(2)}) copy-start(bf16[16,64,256]{2,1,0:T(8,128)(2,1)} %param.10) | copy-start | bytes 1572868
  39.5 30.0 %copy-start.1 = (bf16[14,4096]{1,0:T(8,128)(2,1)S(1)}, bf16[14,4096]{1,0:T(8,128)(2,1)}, u32[]{:S(2)}) copy-start(bf16[14,4096]{1,0:T(8,128)(2,1)} %param.12) | copy-start | bytes 344068

commit v3 on v2

--- a/solution.py
+++ b/solution.py
@@ -57,8 +57,8 @@
     ]
 
 
-def kernel(n, leaves, probes, points, basis, lifts, tops, holders, couplings, coupled, ancestors,
-           pts, tiles, own, got, got_lifts, lifted, spread, unrolled, square, w0, w1, wu, acc,
+def kernel(n, leaves, probes, points, basis, whole_lifts, tops, holders, couplings, coupled, ancestors,
+           pts, tiles, own, lifts, got, got_lifts, lifted, spread, unrolled, square, w0, w1, wu, acc,
            ladder,
            pts_sem, tile_sem, send_sem, recv_sem, up_send, up_recv):
     me = lax.axis_index("leaf")
@@ -79,6 +79,15 @@
     for k in range(CHUNKS):
         point_copy(k).start()
     tile_copy.start()
+
+    new = lax.broadcasted_iota(jnp.int32, (128, 128), 0)
+    old = lax.broadcasted_iota(jnp.int32, (128, 128), 1)
+    halve = jnp.where(old == new // 64 * 64 + new % 32 * 2 + new % 64 // 32, 1.0, 0.0).astype(BF)
+    for at in range(0, whole_lifts.shape[0], 128):
+        rows = min(128, whole_lifts.shape[0] - at)
+        turned = matmul(halve[:rows, :rows], whole_lifts[at:at + rows, :]).astype(BF)
+        lifts[at:at + rows, :] = lax.dot_general(
+            turned, halve, (((1,), (1,)), ((), ())), preferred_element_type=F32).astype(BF)
 
     barrier = pltpu.get_barrier_semaphore()
     greeted = [(None, device) for _, device in partners]
@@ -182,21 +191,39 @@
             unrolled[pl.ds(q, count, stride=32), :] = turn(part)
         square[pl.ds(start + 1, count)] = unrolled[:count * 32, :].astype(BF).reshape(count, 32, 128)
 
-    def open_group(group, turns):
-        def turn(part):
-            return jnp.concatenate(
-                [pltpu.roll(part[u * 8:(u + 1) * 8], turns[u], 1) for u in range(2)], axis=0)
-        open_rows(pl.multiple_of(group * 16, 16), 16, turn)
+    out_row = lax.broadcasted_iota(jnp.int32, (256, 256), 0)
+    in_row = lax.broadcasted_iota(jnp.int32, (256, 256), 1)
+    regroup = jnp.where(in_row == out_row % 16 * 16 + out_row // 16, 1.0, 0.0).astype(BF)
+
+    def open_two(left, right, turned):
+        for half in range(2):
+            stacked = jnp.concatenate([
+                jnp.concatenate([tiles[pl.ds(at, 16), q * 128:(q + 1) * 128]
+                                 for at in (left, right)], axis=1)
+                for q in range(half * 16, half * 16 + 16)], axis=0)
+            opened = matmul(regroup, stacked)
+            for side, at in enumerate((left, right)):
+                part = opened[:, side * 128:(side + 1) * 128]
+                cut = turned[side] * 16
+                if cut == 0:
+                    part = pltpu.roll(part, 64, 1)
+                elif cut < 256:
+                    part = jnp.concatenate([part[:cut], pltpu.roll(part[cut:], 64, 1)], axis=0)
+                square[pl.ds(at + 1, 16), half * 16:half * 16 + 16, :] = (
+                    part.astype(BF).reshape(16, 16, 128))
 
     e0, e1 = 6 * leaves, 3 * leaves
 
-    def open0(group):
-        amount = (group // 3) % 2 * 64
-        open_group(group, (amount, amount))
+    def open0(pair):
+        for u in range(e0 // 32):
+            left = pl.multiple_of(pair * e0 + u * 16, 16)
+            open_two(left, pl.multiple_of(left + e0 // 2, 16), (16, 0))
 
     def open1(step):
-        open_group(step + leaves * 3 * leaves // 16,
-                   ((2 * step // 3) % 2 * 64, ((2 * step + 1) // 3) % 2 * 64))
+        at = pl.multiple_of(leaves * e1 + step * 2 * e1, 16)
+        open_two(at, pl.multiple_of(at + 32, 16), (16, 0))
+        open_two(pl.multiple_of(at + 48, 16), pl.multiple_of(at + 80, 16), (16, 0))
+        open_two(pl.multiple_of(at + 16, 16), pl.multiple_of(at + 64, 16), (8, 8))
 
     def open_upper():
         start = leaves * e1 + (leaves // 2) * (e1 // 2)
@@ -253,7 +280,7 @@
     for i in passed_on:
         arrive(i, CHUNKS)
     for step in range(4):
-        pl.loop(12 * step, 12 * step + 12)(open0)
+        pl.loop(2 * step, 2 * step + 2)(open0)
         if step < CHUNKS - 1:
             for i in passed_on:
                 arrive(i, step)
@@ -261,7 +288,7 @@
             climb_end(step)
     for h in range(4, ups):
         climb_end(h)
-    pl.loop(0, 12)(open1)
+    pl.loop(0, 2)(open1)
     open_upper()
     pl.loop(0, 8)(lambda j: place(w0, 0, j, 16))
     pl.loop(0, 4)(lambda j: place(w1, 1280, j, 8))
@@ -287,10 +314,7 @@
         climb(h).wait_send()
 
 
-def side_by_side(matrices, halved):
-    if halved:
-        split = matrices.reshape(-1, 2, RANK // 2, 2, RANK // 2, 2)
-        return split.transpose(0, 5, 4, 1, 3, 2).reshape(-1, 2 * RANK)
+def side_by_side(matrices):
     return matrices.reshape(-1, 2, RANK, RANK).transpose(0, 3, 1, 2).reshape(-1, 2 * RANK)
 
 
@@ -342,6 +366,7 @@
             pltpu.VMEM(points.shape, BF),
             pltpu.VMEM(couplings.shape, BF),
             pltpu.VMEM((block, probes), BF),
+            pltpu.VMEM((block - RANK, 2 * RANK), BF),
             pltpu.VMEM((count, block, probes), BF),
             pltpu.VMEM((count, block - RANK, 2 * RANK), BF),
             pltpu.VMEM((block - RANK, probes), BF),
@@ -362,8 +387,8 @@
         ],
         compiler_params=pltpu.CompilerParams(
             collective_id=0, has_side_effects=True, vmem_limit_bytes=60 * 2**20),
-    )(points, halved_basis, side_by_side(local_transfer, True),
-      side_by_side(top_transfer, False), holders, couplings)
+    )(points, halved_basis, side_by_side(local_transfer),
+      side_by_side(top_transfer), holders, couplings)
 
 
 def solution(mesh):

time: 147 us -> 82.1 us (0.56)
  local copies, waits for them, and re-layouts: 72.3 us -> 12.4 us
  Pallas kernels: 71.3 us -> 65.5 us
    reshape x2 -> x0, local copies, waits for them, and re-layouts: 37.7 us -> none  [the longest x1 36.4 us: side_by_side(): split = matrices.reshape(-1, 2, RANK // 2, 2, RANK // 2, 2)]
    transpose x1 -> x0, local copies, waits for them, and re-layouts: 27.6 us -> none  [side_by_side(): return split.transpose(0, 5, 4, 1, 3, 2).reshape(-1, 2 * RANK)]
    pallas_call x1, Pallas kernels: 71.3 us -> 65.5 us  [shards(): pl.pallas_call(functools.partial(kernel, n, leaves, probes), out_shape=(j...]
    reshape x3 -> x6, local copies, waits for them, and re-layouts: 1.19 us -> 5.58 us  [side_by_side(): matrices.reshape(-1, 2, RANK, RANK).transpose(0, 3, 1, 2)]
    unnamed x6 -> x2, local copies, waits for them, and re-layouts: 4.69 us -> 4.69 us
where the time goes in v3:
time: 82.1 us; the launch traced here: 80.9 us
  Pallas kernels  65.5 us (80%)
  local copies, waits for them, and re-layouts  12.4 us (15%)
  other arithmetic  2.38 us (3%)
    pallas_call x1, Pallas kernels, shards(): pl.pallas_call(functools.partial(kernel, n, leaves, probes), out_shape=(j...  65.5 us
    reshape x6, local copies, waits for them, and re-layouts, side_by_side(): matrices.reshape(-1, 2, RANK, RANK).transpose(0, 3, 1, 2)  5.58 us
    unnamed x2, local copies, waits for them, and re-layouts  4.69 us
    reshape x2, local copies, waits for them, and re-layouts, shards(): halved_basis = leaf_basis.reshape(leaves, RANK // 2, 2, leaf).swapaxes(1, 2)  2.14 us

profile of v3, /device:TPU:26, one launch (start us, length us, event | category | flops | bytes accessed | tf_op | source)
XLA Modules:
  0.0 80.9 jit_solution(1293214265547677104)
XLA Ops:
  0.6 0.8 fusion
  1.4 1.6 %select_reduce_fusion.holders = s32[1920]{0:T(1024)} fusion(s32[1023]{0:T(1024)S(1)} %get-tuple-element.3, s32[1023]{0:T(1024)S(1)} %get-tuple-element.2), kind=kLoop, calls=%fused_computation | loop fusion | flops 5890560 | bytes 15864 | tf_op jit(solution)/shard_map/reduce_sum | solution.py:342
  3.0 1.1 %reshape.31 = bf16[7,2,64,64]{3,2,1,0:T(8,128)(2,1)S(1)} reshape(bf16[14,4096]{1,0:T(8,128)(2,1)} %param.12) | data formatting | bytes 229376 | tf_op jit(solution)/shard_map/reshape | solution.py:318
  4.2 0.2 copy.16
  4.3 0.8 reshape.32.tops
  5.1 1.4 %reshape.29 = bf16[15,2,64,64]{3,2,1,0:T(8,128)(2,1)S(1)} reshape(bf16[30,4096]{1,0:T(8,128)(2,1)} %param.11) | data formatting | bytes 491520 | tf_op jit(solution)/shard_map/reshape | solution.py:318
  6.6 1.1 %copy.15 = bf16[15,2,64,64]{2,1,3,0:T(2,128)(2,1)S(1)} copy(bf16[15,2,64,64]{3,2,1,0:T(8,128)(2,1)S(1)} %reshape.29) | data formatting | bytes 491520 | tf_op jit(solution)/shard_map/reshape | solution.py:318
  7.7 1.0 %reshape.30.whole_lifts = bf16[960,128]{1,0:T(8,128)(2,1)} reshape(bf16[15,64,2,64]{3,2,1,0:T(2,128)(2,1)S(1)} %bitcast.6) | data formatting | bytes 491520 | tf_op jit(solution)/shard_map/reshape | solution.py:318
  8.6 1.2 %reshape.27 = bf16[16,32,2,256]{3,2,1,0:T(2,128)(2,1)S(1)} reshape(bf16[16,64,256]{2,1,0:T(8,128)(2,1)} %param.10) | data formatting | bytes 1048576 | tf_op jit(solution)/shard_map/reshape | solution.py:351
  9.9 0.9 %copy.14 = bf16[16,32,2,256]{3,1,2,0:T(8,128)(2,1)} copy(bf16[16,32,2,256]{3,2,1,0:T(2,128)(2,1)S(1)} %reshape.27) | data formatting | bytes 1048576 | tf_op jit(solution)/shard_map/reshape | solution.py:351
  10.8 65.5 %shard_map.104 = (bf16[31,64,512]{2,1,0:T(8,128)(2,1)}, bf16[1,3,64,512]{3,2,1,0:T(8,128)(2,1)}) custom-call(bf16[4096,512]{1,0:T(8,128)(2,1)} %points.1, bf16[16,64,256]{2,1,0:T(8,128)(2,1)} %bitcast.5, bf16[960,128]{1,0:T(8,128)(2,1)} %reshape.30.whole_lifts, bf16[448,128]{1,0:T(8,128)(2,1)} %reshape.32.tops, s32[1920]{0:T(1024)} %select_reduce_fusion.holders, ...), custom_call_target="tpu_custom_call" | custom-call | tf_op jit(solution)/shard_map/pallas_call | solution.py:357
  76.2 3.1 %copy.19 = bf16[31,64,512]{2,1,0:T(8,128)(2,1)} copy(bf16[31,64,512]{2,1,0:T(8,128)(2,1)} %get-tuple-element.6) | data formatting | bytes 4063232
  79.3 1.6 %copy.20 = bf16[1,3,64,512]{3,2,1,0:T(8,128)(2,1)} copy(bf16[1,3,64,512]{3,2,1,0:T(8,128)(2,1)} %get-tuple-element.7) | data formatting | bytes 393216

commit v4 on v3

--- a/solution.py
+++ b/solution.py
@@ -57,8 +57,8 @@
     ]
 
 
-def kernel(n, leaves, probes, points, basis, whole_lifts, tops, holders, couplings, coupled, ancestors,
-           pts, tiles, own, lifts, got, got_lifts, lifted, spread, unrolled, square, w0, w1, wu, acc,
+def kernel(n, leaves, probes, points, whole_basis, matrices, holders, couplings, coupled, ancestors,
+           pts, tiles, basis, own, lifts, got, got_lifts, lifted, spread, unrolled, square, w0, w1, wu, acc,
            ladder,
            pts_sem, tile_sem, send_sem, recv_sem, up_send, up_recv):
     me = lax.axis_index("leaf")
@@ -83,9 +83,11 @@
     new = lax.broadcasted_iota(jnp.int32, (128, 128), 0)
     old = lax.broadcasted_iota(jnp.int32, (128, 128), 1)
     halve = jnp.where(old == new // 64 * 64 + new % 32 * 2 + new % 64 // 32, 1.0, 0.0).astype(BF)
-    for at in range(0, whole_lifts.shape[0], 128):
-        rows = min(128, whole_lifts.shape[0] - at)
-        turned = matmul(halve[:rows, :rows], whole_lifts[at:at + rows, :]).astype(BF)
+    for j in range(leaves):
+        basis[j] = matmul(halve[:RANK, :RANK], whole_basis[j]).astype(BF)
+    for at in range(0, lifts.shape[0], 128):
+        rows = min(128, lifts.shape[0] - at)
+        turned = matmul(halve[:rows, :rows], matrices[at:at + rows, :]).astype(BF)
         lifts[at:at + rows, :] = lax.dot_general(
             turned, halve, (((1,), (1,)), ((), ())), preferred_element_type=F32).astype(BF)
 
@@ -163,8 +165,8 @@
     def climb_end(h):
         climb(h).wait_recv()
         pairs = sum(n >> (g + 1) for g in range(h))
-        row = (pairs + me // (1 << (h + 1))) * RANK
-        matrix = tops[pl.ds(pl.multiple_of(row, RANK), RANK), :]
+        row = (leaves - 1 + pairs + me // (1 << (h + 1))) * RANK
+        matrix = matrices[pl.ds(pl.multiple_of(row, RANK), RANK), :]
         both = ladder[h].reshape(2 * RANK, probes)
         value = matmul(matrix, both).astype(BF)
         ancestors[0, h] = value
@@ -344,12 +346,10 @@
 
 def shards(points, leaf_basis, local_transfer, top_transfer, sources, couplings):
     n = lax.axis_size("leaf")
-    leaves, _, leaf = leaf_basis.shape
+    leaves = leaf_basis.shape[0]
     probes = points.shape[1]
     ups = n.bit_length() - 1
     holders = source_holders(sources, lax.axis_index("leaf"), leaves)
-    halved_basis = leaf_basis.reshape(leaves, RANK // 2, 2, leaf).swapaxes(1, 2)
-    halved_basis = halved_basis.reshape(leaves, RANK, leaf)
     block = leaves * RANK
     count = 5 if n == 8 else 4
     vmem = pl.BlockSpec(memory_space=pltpu.VMEM)
@@ -360,11 +360,12 @@
             jax.ShapeDtypeStruct((2 * leaves - 1, RANK, probes), BF),
             jax.ShapeDtypeStruct((1, ups, RANK, probes), BF),
         ),
-        in_specs=[anywhere, vmem, vmem, vmem, pl.BlockSpec(memory_space=pltpu.SMEM), anywhere],
+        in_specs=[anywhere, vmem, vmem, pl.BlockSpec(memory_space=pltpu.SMEM), anywhere],
         out_specs=(vmem, vmem),
         scratch_shapes=[
             pltpu.VMEM(points.shape, BF),
             pltpu.VMEM(couplings.shape, BF),
+            pltpu.VMEM(leaf_basis.shape, BF),
             pltpu.VMEM((block, probes), BF),
             pltpu.VMEM((block - RANK, 2 * RANK), BF),
             pltpu.VMEM((count, block, probes), BF),
@@ -387,8 +388,8 @@
         ],
         compiler_params=pltpu.CompilerParams(
             collective_id=0, has_side_effects=True, vmem_limit_bytes=60 * 2**20),
-    )(points, halved_basis, side_by_side(local_transfer),
-      side_by_side(top_transfer), holders, couplings)
+    )(points, leaf_basis, side_by_side(jnp.concatenate([local_transfer, top_transfer])),
+      holders, couplings)
 
 
 def solution(mesh):

time: 82.1 us -> 78.6 us (0.957)
  local copies, waits for them, and re-layouts: 12.4 us -> 7.76 us
  other arithmetic: 2.38 us -> 3.47 us
    reshape x6 -> x3, local copies, waits for them, and re-layouts: 5.58 us -> 3.08 us  [side_by_side(): matrices.reshape(-1, 2, RANK, RANK).transpose(0, 3, 1, 2)]
    reshape x2 -> x0, local copies, waits for them, and re-layouts: 2.14 us -> none  [shards(): halved_basis = leaf_basis.reshape(leaves, RANK // 2, 2, leaf).swapaxes(1, 2)]
    concatenate x0 -> x1, other arithmetic: none -> 1.08 us  [shards(): jnp.concatenate([local_transfer, top_transfer])]
where the time goes in v4:
time: 78.6 us; the launch traced here: 77.5 us
  Pallas kernels  65.6 us (83%)
  local copies, waits for them, and re-layouts  7.76 us (10%)
  other arithmetic  3.47 us (4%)
    pallas_call x1, Pallas kernels, shards(): pl.pallas_call(functools.partial(kernel, n, leaves, probes), out_shape=(j...  65.6 us
    unnamed x2, local copies, waits for them, and re-layouts  4.69 us
    reshape x3, local copies, waits for them, and re-layouts, side_by_side(): matrices.reshape(-1, 2, RANK, RANK).transpose(0, 3, 1, 2)  3.08 us
    reduce_sum x1, other arithmetic, source_holders(): jnp.where(key[:, None] == slots[None, :], entry[:, None], 0).sum(axis=0)  1.63 us

profile of v4, /device:TPU:26, one launch (start us, length us, event | category | flops | bytes accessed | tf_op | source)
XLA Modules:
  0.0 77.5 jit_solution(14292151647939993938)
XLA Ops:
  0.6 0.8 fusion
  1.4 1.6 %select_reduce_fusion.holders = s32[1920]{0:T(1024)} fusion(s32[1023]{0:T(1024)S(1)} %get-tuple-element.3, s32[1023]{0:T(1024)S(1)} %get-tuple-element.2), kind=kLoop, calls=%fused_computation | loop fusion | flops 5890560 | bytes 15864 | tf_op jit(solution)/shard_map/reduce_sum | solution.py:344
  3.0 1.1 %pad_maximum_fusion = bf16[44,4096]{1,0:T(8,128)(2,1)S(1)} fusion(bf16[14,4096]{1,0:T(8,128)(2,1)} %param.12, bf16[30,4096]{1,0:T(8,128)(2,1)} %param.11), kind=kLoop, calls=%fused_computation.2 | loop fusion | flops 720896 | bytes 720896 | tf_op jit(solution)/shard_map/concatenate | solution.py:391
  4.1 0.8 reshape.15
  4.9 1.2 %copy.12 = bf16[22,2,64,64]{2,1,3,0:T(2,128)(2,1)S(1)} copy(bf16[22,2,64,64]{3,2,1,0:T(8,128)(2,1)S(1)} %reshape.15) | data formatting | bytes 720896 | tf_op jit(solution)/shard_map/reshape | solution.py:320
  6.1 1.1 %reshape.16.matrices = bf16[1408,128]{1,0:T(8,128)(2,1)} reshape(bf16[22,64,2,64]{3,2,1,0:T(2,128)(2,1)S(1)} %bitcast.1) | data formatting | bytes 720896 | tf_op jit(solution)/shard_map/reshape | solution.py:320
  7.2 65.6 %shard_map.104 = (bf16[31,64,512]{2,1,0:T(8,128)(2,1)}, bf16[1,3,64,512]{3,2,1,0:T(8,128)(2,1)}) custom-call(bf16[4096,512]{1,0:T(8,128)(2,1)} %points.1, bf16[16,64,256]{2,1,0:T(8,128)(2,1)} %whole_basis.1, bf16[1408,128]{1,0:T(8,128)(2,1)} %reshape.16.matrices, s32[1920]{0:T(1024)} %select_reduce_fusion.holders, bf16[1023,4096]{1,0:T(8,128)(2,1)} %couplings.1), custom_call_target="tpu_custom_call" | custom-call | tf_op jit(solution)/shard_map/pallas_call | solution.py:357
  72.8 3.1 %copy.15 = bf16[31,64,512]{2,1,0:T(8,128)(2,1)} copy(bf16[31,64,512]{2,1,0:T(8,128)(2,1)} %get-tuple-element.6) | data formatting | bytes 4063232
  75.8 1.6 %copy.16 = bf16[1,3,64,512]{3,2,1,0:T(8,128)(2,1)} copy(bf16[1,3,64,512]{3,2,1,0:T(8,128)(2,1)} %get-tuple-element.7) | data formatting | bytes 393216
